TPU v7x, 32 devices: a whole 2x2x4 slice. The times are simulated.
32 devices in a mesh: gx: 2 (over x), gy: 4 (over z), gz: 4 (over y, core).
Axes of the slice: x: 2, y: 2, z: 4, core: 2. Of those that a mesh axis runs over, the one named last changes fastest.
Arguments:
- snapshots: float32 [4, 4, 4096, 8192], P(None, 'gz', 'gx', 'gy'), may hold values from -6 to 6
- steps: int32 [4], replicated, may hold values from 0 to 3999
- mask: int32 [4, 64], replicated, may hold values 0 or 1
- probe: float32 [4096], replicated, may hold values from -6 to 6
Outputs:
- weights: bfloat16 [4, 4096, 8192], P(None, ('gx', 'gy'), 'gz')
- checks: float32 [4, 64], replicated
All inputs are finite; a program needn't handle non-finite values.
Results may differ from a plain program's by a relative error of at most 0.0029.
Values may be sent and summed in bfloat16 or wider, within the bound.
A program may use at most 256 MiB of HBM per device.

v0:
```python
import math

import jax
import jax.numpy as jnp
from jax import lax
from jax.sharding import PartitionSpec as P

D = 4096
BLOCK = 128


decay_span = 1000.0


def blend_coef(steps):
    expo = jnp.exp(steps.astype(jnp.float32) / decay_span)
    return expo / jnp.sum(expo)


def blend_all(stack, coef):
    acc = coef[0] * stack[0]
    for k in range(1, stack.shape[0]):
        acc = acc + coef[k] * stack[k]
    return acc


def apply_mask(blended, mask_part):
    wide_mask = jnp.repeat(mask_part.astype(jnp.float32), BLOCK, axis=1)
    return (blended * wide_mask[:, None, :]).astype(jnp.bfloat16)


def block_checks(weights, probe_rows):
    per_col = jnp.einsum(
        "d,ldc->lc",
        probe_rows,
        weights,
        preferred_element_type=jnp.float32,
        precision=lax.Precision.HIGHEST,
    )
    layer_count = per_col.shape[0]
    grouped = per_col.reshape(layer_count, per_col.shape[1] // BLOCK, BLOCK)
    return jnp.sum(grouped, axis=2) / math.sqrt(D * BLOCK)


def local(snapshots, steps, mask, probe):
    coef = blend_coef(steps)
    layer_total = mask.shape[0]
    block_total = mask.shape[1]
    empty = jnp.zeros((layer_total, block_total), jnp.float32)
    layer_count = snapshots.shape[1]
    row_count = snapshots.shape[2]
    block_count = snapshots.shape[3] // BLOCK
    layer_start = lax.axis_index("gz") * layer_count
    col_start = lax.axis_index("gy") * block_count
    mask_part = lax.dynamic_slice(mask, (layer_start, col_start), (layer_count, block_count))
    local_weights = apply_mask(blend_all(snapshots, coef), mask_part)
    probe_rows = lax.dynamic_slice_in_dim(probe, lax.axis_index("gx") * row_count, row_count, 0)
    partial_checks = block_checks(local_weights, probe_rows)
    placed = lax.dynamic_update_slice(empty, partial_checks, (layer_start, col_start))
    weights = lax.all_to_all(
        lax.all_to_all(local_weights, "gy", split_axis=1, concat_axis=2, tiled=True),
        "gz",
        split_axis=2,
        concat_axis=0,
        tiled=True,
    )
    checks = lax.psum(placed, ("gx", "gy", "gz"))
    return (weights, checks)


def solution(mesh):
    in_specs = (P(None, "gz", "gx", "gy"), P(), P(), P())
    out_specs = (P(None, ("gx", "gy"), "gz"), P())
    return jax.shard_map(local, mesh=mesh, in_specs=in_specs, out_specs=out_specs, check_vma=False)
```

profile of v0, /device:TPU:12, one launch (start us, length us, event | category | flops | bytes accessed | tf_op | source)
XLA Modules:
  0.0 643.6 jit_solution(18122133762694242894)
XLA Ops:
  0.6 0.0 copy-start
  0.7 0.8 convert_bitcast_fusion
  1.4 0.1 broadcast_bitcast_fusion
  1.5 0.0 copy-start.1
  1.5 45.6 %fusion.11 = (f32[1,1,2048,2048]{3,2,1,0:T(8,128)}, f32[1,1,2048,2048]{3,2,1,0:T(8,128)}, f32[1,1,2048,2048]{3,2,1,0:T(8,128)}, f32[1,1,2048,2048]{3,2,1,0:T(8,128)}) fusion(f32[4,1,2048,2048]{3,2,1,0:T(8,128)} %param.4), kind=kLoop, calls=%fused_computation.21 | loop fusion | bytes 134217728 | tf_op jit(solution)/shard_map/slice | solution.py:21
  47.1 0.0 copy-done.1
  47.1 0.6 fusion.9
  47.7 0.7 broadcast_divide_fusion
  48.4 0.7 fusion.12
  49.1 58.6 %fusion.4 = (bf16[1,2048,2048]{2,0,1:T(2,128)(2,1)}, f32[1,1,2048,2048]{3,0,2,1:T(1,128)}) fusion(f32[2048]{0:T(1024)S(1)} %broadcast_bitcast_fusion, f32[1,1,2048,2048]{3,2,1,0:T(8,128)} %get-tuple-element.15, f32[]{:T(128)} %bitcast.3, f32[1,1,2048,2048]{3,2,1,0:T(8,128)} %get-tuple-element.13, f32[]{:T(128)} %bitcast.2, ...), kind=kLoop, calls=%fused_computation.10 | loop fusion | flops 37748736 | bytes 92282896 | tf_op jit(solution)/shard_map/convert_element_type | solution.py:29
  107.6 0.5 broadcast.106
  108.1 51.2 %reduce.2 = bf16[2048,2048]{1,0:T(8,128)(2,1)} reduce(bf16[2048,1,2048]{2,1,0:T(2,128)(2,1)} %bitcast.52, bf16[]{:T(256)} %broadcast.106), dimensions={1}, to_apply=%bitcast.38.reduce_sub_computation | reduce | bytes 16777218
  159.3 10.0 %reshape.158 = bf16[4,2,524288]{2,1,0:T(2,128)(2,1)} reshape(bf16[2048,2048]{1,0:T(8,128)(2,1)} %reduce.2) | data formatting | bytes 16777216
  169.3 189.6 %all_to_all.36 = bf16[4,2,524288]{2,1,0:T(2,128)(2,1)} all-to-all(bf16[4,2,524288]{2,1,0:T(2,128)(2,1)} %reshape.158), channel_id=1, replica_groups=mesh['gx'=2,'gy'=4,'gz'=4] {'gy'}, dimensions={0} | all-to-all | bytes 16777216 | tf_op jit(solution)/shard_map/all_to_all | solution.py:61
  358.8 12.3 %reshape.159 = bf16[2048,1,2048]{2,1,0:T(2,128)(2,1)} reshape(bf16[4,2,524288]{2,1,0:T(2,128)(2,1)} %all_to_all.36) | data formatting | bytes 16777216
  371.2 13.5 %copy.25 = bf16[1,2048,2048]{2,1,0:T(8,128)(2,1)} copy(bf16[1,2048,2048]{2,0,1:T(2,128)(2,1)} %bitcast.49) | data formatting | bytes 16777216
  384.6 11.4 %copy.20 = bf16[1,512,4,2048]{1,3,2,0:T(8,128)(2,1)} copy(bf16[1,512,4,2048]{3,1,2,0:T(8,128)(2,1)} %bitcast.53) | data formatting | bytes 16777216 | tf_op jit(solution)/shard_map/all_to_all | solution.py:61
  396.0 15.5 %copy.63 = bf16[1,512,8192]{1,0,2:T(2,128)(2,1)} copy(bf16[1,512,8192]{1,2,0:T(8,128)(2,1)} %bitcast.54) | data formatting | bytes 16777216 | tf_op jit(solution)/shard_map/all_to_all | solution.py:61
  411.5 54.8 %reduce.3 = bf16[8192,512]{1,0:T(8,128)(2,1)} reduce(bf16[8192,1,512]{2,1,0:T(2,128)(2,1)} %bitcast.51, bf16[]{:T(256)} %broadcast.106), dimensions={1}, to_apply=%bitcast.48.reduce_sub_computation | reduce | bytes 16777218
  466.2 9.9 %reshape.160 = bf16[4,2,524288]{2,1,0:T(2,128)(2,1)} reshape(bf16[8192,512]{1,0:T(8,128)(2,1)} %reduce.3) | data formatting | bytes 16777216
  476.2 6.1 all-to-all-start.1
  482.3 0.0 copy-done
  482.3 14.4 %fusion.6 = f32[1,16,128]{2,0,1:T(1,128)S(1)} fusion(f32[2048,1,1]{0,1,2:T(1,128)S(1)} %bitcast.56, f32[1,1,2048,2048]{3,0,2,1:T(1,128)} %get-tuple-element.11, f32[2048]{0:T(1024)S(1)} %broadcast_bitcast_fusion), kind=kOutput, calls=%fused_computation.12 | convolution fusion | flops 58720256 | bytes 16801792 | tf_op jit(solution)/shard_map/d,ldc->lc/dot_general | solution.py:33
  496.7 0.1 reduce_sum.19
  496.8 0.3 dynamic_update_slice.3
  497.1 111.2 %psum.7 = f32[4,64]{1,0:T(4,128)} all-reduce(f32[4,64]{1,0:T(4,128)S(1)} %dynamic_update_slice.3), channel_id=1, replica_groups=mesh['gx'=2,'gy'=4,'gz'=4] {'gx','gy','gz'}, use_global_device_ids=true, to_apply=%region_2.0 | all-reduce | flops 256 | bytes 2048 | tf_op jit(solution)/shard_map/psum | solution.py:67
  608.3 0.0 all-to-all-done.1
  608.3 12.3 %reshape.161 = bf16[8192,1,512]{2,1,0:T(2,128)(2,1)} reshape(bf16[4,2,524288]{2,1,0:T(2,128)(2,1)} %all-to-all-done.1) | data formatting | bytes 16777216
  620.7 11.6 %copy.26 = bf16[1,512,8192]{1,2,0:T(8,128)(2,1)} copy(bf16[1,512,8192]{1,0,2:T(2,128)(2,1)} %bitcast.50) | data formatting | bytes 16777216
  632.3 11.3 %copy.22 = bf16[4,512,2048]{2,1,0:T(8,128)(2,1)} copy(bf16[4,512,2048]{1,2,0:T(8,128)(2,1)} %bitcast.55) | data formatting | bytes 16777216
  (3 shorter events, 0.0 us)
Async XLA Ops:
  0.6 481.6 %copy-start = (f32[4096]{0:T(1024)S(1)}, f32[4096]{0:T(1024)}, u32[]{:S(2)}) copy-start(f32[4096]{0:T(1024)} %param.7) | copy-start | bytes 49156
  1.5 45.6 %copy-start.1 = (s32[4]{0:T(128)S(1)}, s32[4]{0:T(128)}, u32[]{:S(2)}) copy-start(s32[4]{0:T(128)} %param.5) | copy-start | bytes 52
  476.2 132.2 %all-to-all-start.1 = ((bf16[4,2,524288]{2,1,0:T(2,128)(2,1)}), bf16[4,2,524288]{2,1,0:T(2,128)(2,1)}, u32[]{:S(2)}, u32[]{:S(2)}) async-start(bf16[4,2,524288]{2,1,0:T(2,128)(2,1)} %reshape.160), calls=%async_computation.1 | async-start | bytes 16777216 | tf_op jit(solution)/shard_map/all_to_all | solution.py:60
where the time goes:
time: 647 us; the launch traced here: 644 us
  blocking collectives  301 us (47%)
  other arithmetic  167 us (26%)
  local copies, waits for them, and re-layouts  155 us (24%)
  matrix products  14.4 us (2%)
    all_to_all x1, blocking collectives, local(): lax.all_to_all(local_weights, 'gy', split_axis=1, concat_axis=2, tiled=True)  190 us
    psum x1, blocking collectives, local(): checks = lax.psum(placed, ('gx', 'gy', 'gz'))  111 us
    unnamed x2, other arithmetic  106 us
    unnamed x12, local copies, waits for them, and re-layouts  81.5 us
    convert_element_type x1, other arithmetic, apply_mask(): return (blended * wide_mask[:, None, :]).astype(jnp.bfloat16)  58.6 us
    slice x2, local copies, waits for them, and re-layouts, blend_all(): acc = coef[0] * stack[0]  46.3 us
    all_to_all x2, local copies, waits for them, and re-layouts, local(): lax.all_to_all(local_weights, 'gy', split_axis=1, concat_axis=2, tiled=True)  26.9 us
    dot_general x1, matrix products, block_checks(): jnp.einsum('d,ldc->lc', probe_rows, weights, preferred_element_type=jnp.f...  14.4 us
  transfers between devices with their start and end apart: 1, of which 0 were waited for; matrix products, arithmetic and copies ran while one was open for 2% of the time, Pallas kernels for 0%

commit v1 on v0

v1 whole, which is shorter than its diff:
```python
import functools
import math

import jax
import jax.numpy as jnp
from jax import lax
from jax.experimental import pallas as pl
from jax.experimental.pallas import tpu as pltpu
from jax.sharding import PartitionSpec as P

MESH = pl.DeviceIdType.MESH
BLOCK = 128
CORES = 2
CHUNK = 64
STRIP = 16
FETCH = 3
decay_span = 1000.0


def kernel(dims, snap_ref, steps_ref, mask_ref, probe_ref, land_ref, checks_ref,
           fetched, held, coef, acc, xtile, gtile,
           fetch_sem, send_sem, relay_sem, land_sem,
           xsend_sem, xland_sem, gsend_sem, gland_sem):
    nx, ny, nz, norm = dims
    snaps, _, rows, cols = snap_ref.shape
    layers = mask_ref.shape[0]
    nb = cols // BLOCK
    part = rows // ny
    chunk = fetched.shape[2]
    per = part // chunk
    steps_total = ny * per
    pairs = nz // CORES

    x = lax.axis_index("gx")
    g = lax.axis_index("gy")
    l = lax.axis_index("gz")
    me = g * nz + l
    group = ny * nz
    low = 1 - g // (ny // 2)

    def quarter(t):
        j = t % ny
        return j + low * (ny - 1 - 2 * j)

    def fetch(t):
        row = pl.multiple_of(quarter(t) * part + (t // ny) * chunk, chunk)
        slot = t % FETCH
        return pltpu.make_async_copy(
            snap_ref.at[:, 0, pl.ds(row, chunk), :], fetched.at[slot], fetch_sem.at[slot]
        )

    for t in range(min(FETCH - 1, steps_total)):
        fetch(t).start()

    barrier = pltpu.get_barrier_semaphore()

    def greet_group(i, carry):
        other = (me + i) % group
        pl.semaphore_signal(
            barrier, inc=1, device_id={"gy": other // nz, "gz": other % nz}, device_id_type=MESH
        )
        return carry

    def greet_line(i, carry):
        pl.semaphore_signal(barrier, inc=1, device_id={"gx": (x + i) % nx}, device_id_type=MESH)
        return carry

    lax.fori_loop(1, group, greet_group, 0)
    lax.fori_loop(1, nx, greet_line, 0)

    expos = [
        jnp.exp(jnp.full((1, cols), steps_ref[k], jnp.int32).astype(jnp.float32) / decay_span)
        for k in range(snaps)
    ]
    total = expos[0]
    for k in range(1, snaps):
        total = total + expos[k]
    for b in range(nb):
        keep = jnp.full((1, BLOCK), mask_ref[l, g * nb + b], jnp.int32).astype(jnp.float32)
        lanes = slice(b * BLOCK, (b + 1) * BLOCK)
        for k in range(snaps):
            coef[k, :, lanes] = (expos[k][:, lanes] / total[:, lanes]) * keep
    acc[...] = jnp.zeros_like(acc)

    pl.semaphore_wait(barrier, group - 1 + nx - 1)

    ahead = (g // CORES - l // CORES + pairs) % pairs
    final = ahead == 0
    relay_core = (l // CORES) * CORES + g % CORES
    slot_out = jnp.where(final, l, layers + CORES * (ahead - 1) + l % CORES)

    def step(t, carry):
        @pl.when(t + (FETCH - 1) < steps_total)
        def _():
            fetch(t + (FETCH - 1)).start()

        fetch(t).wait()
        slot = t % FETCH
        r = quarter(t)
        k = t // ny
        base = pl.multiple_of(k * chunk, chunk)

        def strip(i, inner):
            off = pl.multiple_of(i * STRIP, STRIP)
            here = pl.ds(off, STRIP)
            mixed = coef[0] * fetched[slot, 0, here, :]
            for s in range(1, snaps):
                mixed = mixed + coef[s] * fetched[slot, s, here, :]
            value = mixed.astype(jnp.bfloat16)
            held[r, pl.ds(pl.multiple_of(base + off, STRIP), STRIP), :] = value
            weight = probe_ref[pl.ds(pl.multiple_of(r * part + base + off, STRIP), STRIP), :]
            term = value.astype(jnp.float32) * weight
            acc[...] += term[:8] + term[8:]
            return inner

        lax.fori_loop(0, chunk // STRIP, strip, 0)

        source = held.at[r, pl.ds(base, chunk), :]
        target = land_ref.at[slot_out, pl.ds(base, chunk), :]
        stays = jnp.logical_and(r == g, relay_core == l)

        @pl.when(stays)
        def _():
            pltpu.make_async_copy(source, target, land_sem.at[slot_out, k]).start()

        @pl.when(jnp.logical_not(stays))
        def _():
            pltpu.make_async_remote_copy(
                src_ref=source,
                dst_ref=target,
                send_sem=send_sem.at[r, k],
                recv_sem=land_sem.at[slot_out, k],
                device_id={"gy": r, "gz": relay_core},
                device_id_type=MESH,
            ).start()

        return carry

    lax.fori_loop(0, steps_total, step, 0)

    def xcopy(i, slot):
        return pltpu.make_async_remote_copy(
            src_ref=xtile.at[slot],
            dst_ref=xtile.at[slot],
            send_sem=xsend_sem.at[i],
            recv_sem=xland_sem.at[slot],
            device_id={"gx": (x + i) % nx},
            device_id_type=MESH,
        )

    def gcopy(i, slot):
        other = (me + i) % group
        return pltpu.make_async_remote_copy(
            src_ref=gtile.at[slot],
            dst_ref=gtile.at[slot],
            send_sem=gsend_sem.at[i],
            recv_sem=gland_sem.at[slot],
            device_id={"gy": other // nz, "gz": other % nz},
            device_id_type=MESH,
        )

    def each(low_end, high_end, action):
        def body(i, carry):
            action(i)
            return carry

        lax.fori_loop(low_end, high_end, body, 0)

    tile = jnp.zeros(xtile.shape[1:], jnp.float32)
    row_id = lax.broadcasted_iota(jnp.int32, tile.shape, 0)
    lane_id = lax.broadcasted_iota(jnp.int32, tile.shape, 1)
    for b in range(nb):
        part_sum = jnp.sum(acc[:, b * BLOCK:(b + 1) * BLOCK], axis=(0, 1), keepdims=True)
        place = jnp.logical_and(row_id == l, lane_id == g * nb + b)
        tile = tile + jnp.where(place, part_sum, 0.0)
    xtile[x] = tile
    each(1, nx, lambda i: xcopy(i, x).start())

    def relay(ahead_by, core, k):
        goal = CORES * ((l // CORES + ahead_by) % pairs) + l % CORES
        layer = (l // CORES) * CORES + core
        slot = layers + CORES * (ahead_by - 1) + core
        here = pl.ds(pl.multiple_of(k * chunk, chunk), chunk)
        return pltpu.make_async_remote_copy(
            src_ref=land_ref.at[slot, here, :],
            dst_ref=land_ref.at[layer, here, :],
            send_sem=relay_sem.at[slot - layers, k],
            recv_sem=land_sem.at[layer, k],
            device_id={"gz": goal},
            device_id_type=MESH,
        )

    def landed(slot, k):
        here = pl.ds(pl.multiple_of(k * chunk, chunk), chunk)
        return pltpu.make_async_copy(
            land_ref.at[slot, here, :], land_ref.at[slot, here, :], land_sem.at[slot, k]
        )

    def forward(k):
        for ahead_by in range(1, pairs):
            for core in range(CORES):
                landed(layers + CORES * (ahead_by - 1) + core, k).wait()
                relay(ahead_by, core, k).start()

    half = per // 2
    each(0, half, forward)

    each(1, nx, lambda i: xcopy(i, (x + i) % nx).wait_recv())
    line = xtile[0]
    for i in range(1, nx):
        line = line + xtile[i]
    gtile[me] = line
    each(1, group, lambda i: gcopy(i, me).start())

    each(half, per, forward)

    each(1, group, lambda i: gcopy(i, (me + i) % group).wait_recv())
    whole = gtile[0]
    for i in range(1, group):
        whole = whole + gtile[i]
    checks_ref[...] = whole[: checks_ref.shape[0], : checks_ref.shape[1]] / norm

    each(1, nx, lambda i: xcopy(i, x).wait_send())
    each(1, group, lambda i: gcopy(i, me).wait_send())

    def sent(t):
        r = quarter(t)
        k = t // ny
        base = pl.multiple_of(k * chunk, chunk)

        @pl.when(jnp.logical_not(jnp.logical_and(r == g, relay_core == l)))
        def _():
            pltpu.make_async_remote_copy(
                src_ref=held.at[r, pl.ds(base, chunk), :],
                dst_ref=land_ref.at[slot_out, pl.ds(base, chunk), :],
                send_sem=send_sem.at[r, k],
                recv_sem=land_sem.at[slot_out, k],
                device_id={"gy": r, "gz": relay_core},
                device_id_type=MESH,
            ).wait_send()

    each(0, steps_total, sent)

    def relayed(k):
        for ahead_by in range(1, pairs):
            for core in range(CORES):
                relay(ahead_by, core, k).wait_send()

    each(0, per, relayed)

    def arrived(k):
        for layer in range(layers):
            landed(layer, k).wait()

    each(0, per, arrived)


def fused(nx, ny, nz, snapshots, steps, mask, probe):
    snaps, _, rows, cols = snapshots.shape
    layers, blocks = mask.shape
    part = rows // ny
    chunk = min(CHUNK, part)
    per = part // chunk
    pairs = nz // CORES
    spare = CORES * (pairs - 1)
    group = ny * nz
    tile = (-(-layers // 8) * 8, -(-blocks // BLOCK) * BLOCK)
    norm = math.sqrt(rows * nx * BLOCK)
    probe_rows = lax.dynamic_slice_in_dim(probe, lax.axis_index("gx") * rows, rows, 0)
    dma = pltpu.SemaphoreType.DMA
    land, checks = pl.pallas_call(
        functools.partial(kernel, (nx, ny, nz, norm)),
        out_shape=(
            jax.ShapeDtypeStruct((layers + spare, part, cols), jnp.bfloat16),
            jax.ShapeDtypeStruct((layers, blocks), jnp.float32),
        ),
        in_specs=[
            pl.BlockSpec(memory_space=pltpu.HBM),
            pl.BlockSpec(memory_space=pltpu.SMEM),
            pl.BlockSpec(memory_space=pltpu.SMEM),
            pl.BlockSpec(memory_space=pltpu.VMEM),
        ],
        out_specs=(
            pl.BlockSpec(memory_space=pltpu.HBM),
            pl.BlockSpec(memory_space=pltpu.VMEM),
        ),
        scratch_shapes=[
            pltpu.VMEM((FETCH, snaps, chunk, cols), jnp.float32),
            pltpu.VMEM((ny, part, cols), jnp.bfloat16),
            pltpu.VMEM((snaps, 1, cols), jnp.float32),
            pltpu.VMEM((8, cols), jnp.float32),
            pltpu.VMEM((nx,) + tile, jnp.float32),
            pltpu.VMEM((group,) + tile, jnp.float32),
            dma((FETCH,)),
            dma((ny, per)),
            dma((max(spare, 1), per)),
            dma((layers + spare, per)),
            dma((nx,)),
            dma((nx,)),
            dma((group,)),
            dma((group,)),
        ],
        compiler_params=pltpu.CompilerParams(
            collective_id=0, has_side_effects=True, vmem_limit_bytes=48 * 1024 * 1024
        ),
        cost_estimate=pl.CostEstimate(
            flops=10 * snapshots.size // snaps,
            bytes_accessed=4 * snapshots.size + 2 * layers * part * cols,
            transcendentals=0,
        ),
    )(snapshots, steps, mask, probe_rows.reshape(rows, 1))
    return land[:layers], checks


def solution(mesh):
    nx, ny, nz = (mesh.shape[name] for name in ("gx", "gy", "gz"))
    in_specs = (P(None, "gz", "gx", "gy"), P(), P(), P())
    out_specs = (P(None, ("gx", "gy"), "gz"), P())
    assert ny == nz and ny % CORES == 0
    return jax.shard_map(
        functools.partial(fused, nx, ny, nz),
        mesh=mesh, in_specs=in_specs, out_specs=out_specs, check_vma=False,
    )
```

time: 647 us -> 209 us (0.32)
  blocking collectives: 301 us -> 0 us
  Pallas kernels: 0 us -> 196 us
  other arithmetic: 167 us -> 0 us
  local copies, waits for them, and re-layouts: 155 us -> 11.4 us
  matrix products: 14.4 us -> 0 us
    pallas_call x0 -> x1, Pallas kernels: none -> 196 us  [fused(): pl.pallas_call(functools.partial(kernel, (nx, ny, nz, norm)), out_shape=(...]
    all_to_all x1 -> x0, blocking collectives: 190 us -> none  [local(): lax.all_to_all(local_weights, 'gy', split_axis=1, concat_axis=2, tiled=True)]
    psum x1 -> x0, blocking collectives: 111 us -> none  [local(): checks = lax.psum(placed, ('gx', 'gy', 'gz'))]
    unnamed x2 -> x0, other arithmetic: 106 us -> none
    unnamed x12 -> x5, local copies, waits for them, and re-layouts: 81.5 us -> 1.91 us
    convert_element_type x2 -> x0, other arithmetic: 59.3 us -> none  [the longest x1 58.6 us: apply_mask(): return (blended * wide_mask[:, None, :]).astype(jnp.bfloat16)]
    slice x2 -> x1, local copies, waits for them, and re-layouts: 46.3 us -> 8.44 us  [fused(): return (land[:layers], checks)]
    all_to_all x2 -> x0, local copies, waits for them, and re-layouts: 26.9 us -> none  [local(): lax.all_to_all(local_weights, 'gy', split_axis=1, concat_axis=2, tiled=True)]
  transfers between devices with their start and end apart: 1 -> 0, of which waited for: 0 -> 0; matrix products, arithmetic and copies ran while one was open for 2% -> 0% of each run, Pallas kernels for 0% -> 0%
where the time goes in v1:
time: 209 us
  Pallas kernels  196 us (94%)
  local copies, waits for them, and re-layouts  11.4 us (5%)
    pallas_call x1, Pallas kernels, fused(): pl.pallas_call(functools.partial(kernel, (nx, ny, nz, norm)), out_shape=(...  196 us
    slice x1, local copies, waits for them, and re-layouts, fused(): return (land[:layers], checks)  8.44 us

profile of v1, /device:TPU:12, one launch (start us, length us, event | category | flops | bytes accessed | tf_op | source)
XLA Modules:
  0.0 208.5 jit_solution(12492578625149580651)
XLA Ops:
  0.6 0.7 dynamic_slice.3
  1.3 0.4 copy.6.probe_ref
  1.7 0.0 copy-start
  1.7 0.7 copy-done
  2.4 0.0 copy-start.1
  2.4 0.7 copy-done.1
  3.1 196.5 %shard_map.59 = (bf16[6,512,2048]{2,1,0:T(8,128)(2,1)}, f32[4,64]{1,0:T(4,128)S(1)}) custom-call(f32[4,1,2048,2048]{3,2,1,0:T(8,128)} %snap_ref.1, s32[4]{0:T(128)S(1)} %copy-done.1, s32[4,64]{1,0:T(4,128)S(1)} %copy-done, f32[2048,1]{1,0:T(8,128)S(1)} %copy.6.probe_ref), custom_call_target="tpu_custom_call" | custom-call | flops 41943040 | bytes 75497472 | tf_op jit(solution)/shard_map/pallas_call | solution.py:271
  199.5 8.4 %slice.3 = bf16[4,512,2048]{2,1,0:T(8,128)(2,1)} slice(bf16[6,512,2048]{2,1,0:T(8,128)(2,1)} %get-tuple-element.4), slice={[0:4], [0:512], [0:2048]} | slice | bytes 16777216 | tf_op jit(solution)/shard_map/slice | solution.py:312
  208.0 0.6 copy.8
Async XLA Ops:
  1.7 0.7 copy-start
  2.4 0.7 copy-start.1

commit v2 on v1

--- a/solution.py
+++ b/solution.py
@@ -11,19 +11,19 @@
 MESH = pl.DeviceIdType.MESH
 BLOCK = 128
 CORES = 2
-CHUNK = 64
+CHUNK = 32
 STRIP = 16
 FETCH = 3
 decay_span = 1000.0
 
 
-def kernel(dims, snap_ref, steps_ref, mask_ref, probe_ref, land_ref, checks_ref,
+def kernel(dims, snap_ref, steps_hbm, mask_hbm, probe_hbm, land_ref, checks_ref,
            fetched, held, coef, acc, xtile, gtile,
-           fetch_sem, send_sem, relay_sem, land_sem,
+           steps_ref, mask_ref, probe_flat, probe_ref, small_sem, fetch_sem, send_sem, relay_sem, land_sem,
            xsend_sem, xland_sem, gsend_sem, gland_sem):
     nx, ny, nz, norm = dims
     snaps, _, rows, cols = snap_ref.shape
-    layers = mask_ref.shape[0]
+    layers = mask_hbm.shape[0]
     nb = cols // BLOCK
     part = rows // ny
     chunk = fetched.shape[2]
@@ -37,9 +37,10 @@
     me = g * nz + l
     group = ny * nz
     low = 1 - g // (ny // 2)
+    first = jnp.where(jnp.logical_or(g == 0, g == ny - 1), ny // 2, 0)
 
     def quarter(t):
-        j = t % ny
+        j = (t + first) % ny
         return j + low * (ny - 1 - 2 * j)
 
     def fetch(t):
@@ -49,6 +50,13 @@
             snap_ref.at[:, 0, pl.ds(row, chunk), :], fetched.at[slot], fetch_sem.at[slot]
         )
 
+    small = [
+        pltpu.make_async_copy(steps_hbm, steps_ref, small_sem.at[0]),
+        pltpu.make_async_copy(mask_hbm, mask_ref, small_sem.at[1]),
+        pltpu.make_async_copy(probe_hbm, probe_flat, small_sem.at[2]),
+    ]
+    for copy in small:
+        copy.start()
     for t in range(min(FETCH - 1, steps_total)):
         fetch(t).start()
 
@@ -68,6 +76,8 @@
     lax.fori_loop(1, group, greet_group, 0)
     lax.fori_loop(1, nx, greet_line, 0)
 
+    for copy in small:
+        copy.wait()
     expos = [
         jnp.exp(jnp.full((1, cols), steps_ref[k], jnp.int32).astype(jnp.float32) / decay_span)
         for k in range(snaps)
@@ -81,6 +91,9 @@
         for k in range(snaps):
             coef[k, :, lanes] = (expos[k][:, lanes] / total[:, lanes]) * keep
     acc[...] = jnp.zeros_like(acc)
+    for q in range(rows // BLOCK):
+        flat = probe_flat[pl.ds(x * (rows // BLOCK) + q, 1), :]
+        probe_ref[q * BLOCK:(q + 1) * BLOCK, :] = jnp.broadcast_to(flat, (BLOCK, BLOCK)).T
 
     pl.semaphore_wait(barrier, group - 1 + nx - 1)
 
@@ -109,7 +122,7 @@
             value = mixed.astype(jnp.bfloat16)
             held[r, pl.ds(pl.multiple_of(base + off, STRIP), STRIP), :] = value
             weight = probe_ref[pl.ds(pl.multiple_of(r * part + base + off, STRIP), STRIP), :]
-            term = value.astype(jnp.float32) * weight
+            term = value.astype(jnp.float32) * jnp.concatenate([weight] * nb, axis=1)
             acc[...] += term[:8] + term[8:]
             return inner
 
@@ -255,6 +268,18 @@
     each(0, per, arrived)
 
 
+def place(land_ref, sums_ref, weights_ref, checks_ref, sem):
+    copies = [pltpu.make_async_copy(sums_ref, checks_ref, sem.at[weights_ref.shape[0]])]
+    copies += [
+        pltpu.make_async_copy(land_ref.at[layer], weights_ref.at[layer], sem.at[layer])
+        for layer in range(weights_ref.shape[0])
+    ]
+    for copy in copies:
+        copy.start()
+    for copy in copies:
+        copy.wait()
+
+
 def fused(nx, ny, nz, snapshots, steps, mask, probe):
     snaps, _, rows, cols = snapshots.shape
     layers, blocks = mask.shape
@@ -266,22 +291,21 @@
     group = ny * nz
     tile = (-(-layers // 8) * 8, -(-blocks // BLOCK) * BLOCK)
     norm = math.sqrt(rows * nx * BLOCK)
-    probe_rows = lax.dynamic_slice_in_dim(probe, lax.axis_index("gx") * rows, rows, 0)
     dma = pltpu.SemaphoreType.DMA
     land, checks = pl.pallas_call(
         functools.partial(kernel, (nx, ny, nz, norm)),
         out_shape=(
-            jax.ShapeDtypeStruct((layers + spare, part, cols), jnp.bfloat16),
-            jax.ShapeDtypeStruct((layers, blocks), jnp.float32),
+            pltpu.VMEM((layers + spare, part, cols), jnp.bfloat16),
+            pltpu.VMEM((layers, blocks), jnp.float32),
         ),
         in_specs=[
             pl.BlockSpec(memory_space=pltpu.HBM),
-            pl.BlockSpec(memory_space=pltpu.SMEM),
-            pl.BlockSpec(memory_space=pltpu.SMEM),
-            pl.BlockSpec(memory_space=pltpu.VMEM),
+            pl.BlockSpec(memory_space=pltpu.HBM),
+            pl.BlockSpec(memory_space=pltpu.HBM),
+            pl.BlockSpec(memory_space=pltpu.HBM),
         ],
         out_specs=(
-            pl.BlockSpec(memory_space=pltpu.HBM),
+            pl.BlockSpec(memory_space=pltpu.VMEM),
             pl.BlockSpec(memory_space=pltpu.VMEM),
         ),
         scratch_shapes=[
@@ -291,6 +315,11 @@
             pltpu.VMEM((8, cols), jnp.float32),
             pltpu.VMEM((nx,) + tile, jnp.float32),
             pltpu.VMEM((group,) + tile, jnp.float32),
+            pltpu.SMEM(steps.shape, jnp.int32),
+            pltpu.SMEM(mask.shape, jnp.int32),
+            pltpu.VMEM((probe.size // BLOCK, BLOCK), jnp.float32),
+            pltpu.VMEM((rows, BLOCK), jnp.float32),
+            dma((3,)),
             dma((FETCH,)),
             dma((ny, per)),
             dma((max(spare, 1), per)),
@@ -308,8 +337,19 @@
             bytes_accessed=4 * snapshots.size + 2 * layers * part * cols,
             transcendentals=0,
         ),
-    )(snapshots, steps, mask, probe_rows.reshape(rows, 1))
-    return land[:layers], checks
+    )(snapshots, steps, mask, probe.reshape(-1, BLOCK))
+    weights, checks = pl.pallas_call(
+        place,
+        out_shape=(
+            jax.ShapeDtypeStruct((layers, part, cols), jnp.bfloat16),
+            jax.ShapeDtypeStruct((layers, blocks), jnp.float32),
+        ),
+        in_specs=[pl.BlockSpec(memory_space=pltpu.VMEM)] * 2,
+        out_specs=(pl.BlockSpec(memory_space=pltpu.HBM),) * 2,
+        scratch_shapes=[dma((layers + 1,))],
+        compiler_params=pltpu.CompilerParams(vmem_limit_bytes=24 * 1024 * 1024),
+    )(land, checks)
+    return weights, checks
 
 
 def solution(mesh):

time: 209 us -> 198 us (0.947)
  local copies, waits for them, and re-layouts: 11.4 us -> 0 us
    slice x1 -> x0, local copies, waits for them, and re-layouts: 8.44 us -> none  [fused(): return (land[:layers], checks)]
    pallas_call x0 -> x1, Pallas kernels: none -> 3.38 us  [fused(): pl.pallas_call(place, out_shape=(jax.ShapeDtypeStruct((layers, part, cols...]
    pallas_call x1, Pallas kernels: 196 us -> 194 us  [fused(): pl.pallas_call(functools.partial(kernel, (nx, ny, nz, norm)), out_shape=(...]
where the time goes in v2:
time: 198 us
  Pallas kernels  197 us (99%)
    pallas_call x1, Pallas kernels, fused(): pl.pallas_call(functools.partial(kernel, (nx, ny, nz, norm)), out_shape=(...  194 us

profile of v2, /device:TPU:12, one launch (start us, length us, event | category | flops | bytes accessed | tf_op | source)
XLA Modules:
  0.0 197.5 jit_solution(794278247174872370)
XLA Ops:
  0.6 193.5 %shard_map.59 = (bf16[6,512,2048]{2,1,0:T(8,128)(2,1)S(1)}, f32[4,64]{1,0:T(4,128)S(1)}) custom-call(f32[4,1,2048,2048]{3,2,1,0:T(8,128)} %snap_ref.1, s32[4]{0:T(128)} %steps_hbm.1, s32[4,64]{1,0:T(4,128)} %mask_hbm.1, f32[32,128]{1,0:T(8,128)} %bitcast.1), custom_call_target="tpu_custom_call" | custom-call | flops 41943040 | bytes 75497472 | tf_op jit(solution)/shard_map/pallas_call | solution.py:295
  194.2 3.4 %shard_map.60 = (bf16[4,512,2048]{2,1,0:T(8,128)(2,1)}, f32[4,64]{1,0:T(4,128)}) custom-call(bf16[6,512,2048]{2,1,0:T(8,128)(2,1)S(1)} %get-tuple-element.4.land_ref, f32[4,64]{1,0:T(4,128)S(1)} %get-tuple-element.5.sums_ref), custom_call_target="tpu_custom_call" | custom-call | tf_op jit(solution)/shard_map/pallas_call | solution.py:341

commit v3 on v2

--- a/solution.py
+++ b/solution.py
@@ -37,14 +37,30 @@
     me = g * nz + l
     group = ny * nz
     low = 1 - g // (ny // 2)
-    first = jnp.where(jnp.logical_or(g == 0, g == ny - 1), ny // 2, 0)
-
-    def quarter(t):
-        j = (t + first) % ny
-        return j + low * (ny - 1 - 2 * j)
+    edge = jnp.logical_or(g == 0, g == ny - 1)
+    across = ny // 2
+    near = ny - 1 - across
+    near_end = near * per
+    across_end = near_end + across * per
+
+    def place_of(t):
+        wide = max(near, 1)
+        later = t - near_end
+        in_near = t < near_end
+        in_across = t < across_end
+        edge_j = jnp.where(
+            in_near, across + t % wide, jnp.where(in_across, later % across, ny - 1)
+        )
+        edge_k = jnp.where(
+            in_near, t // wide, jnp.where(in_across, later // across, t - across_end)
+        )
+        j = jnp.where(edge, edge_j, t % ny)
+        k = jnp.where(edge, edge_k, t // ny)
+        return j + low * (ny - 1 - 2 * j), k
 
     def fetch(t):
-        row = pl.multiple_of(quarter(t) * part + (t // ny) * chunk, chunk)
+        r, k = place_of(t)
+        row = pl.multiple_of(r * part + k * chunk, chunk)
         slot = t % FETCH
         return pltpu.make_async_copy(
             snap_ref.at[:, 0, pl.ds(row, chunk), :], fetched.at[slot], fetch_sem.at[slot]
@@ -109,8 +125,7 @@
 
         fetch(t).wait()
         slot = t % FETCH
-        r = quarter(t)
-        k = t // ny
+        r, k = place_of(t)
         base = pl.multiple_of(k * chunk, chunk)
 
         def strip(i, inner):
@@ -237,8 +252,7 @@
     each(1, group, lambda i: gcopy(i, me).wait_send())
 
     def sent(t):
-        r = quarter(t)
-        k = t // ny
+        r, k = place_of(t)
         base = pl.multiple_of(k * chunk, chunk)
 
         @pl.when(jnp.logical_not(jnp.logical_and(r == g, relay_core == l)))

time: 198 us -> 198 us (level)
  no operation moved by 1% of the time
where the time goes in v3:
time: 198 us
  Pallas kernels  197 us (99%)
    pallas_call x1, Pallas kernels, fused(): pl.pallas_call(functools.partial(kernel, (nx, ny, nz, norm)), out_shape=(...  194 us

profile of v3, /device:TPU:12, one launch (start us, length us, event | category | flops | bytes accessed | tf_op | source)
XLA Modules:
  0.0 197.9 jit_solution(3783659337156825945)
XLA Ops:
  0.6 193.9 %shard_map.59 = (bf16[6,512,2048]{2,1,0:T(8,128)(2,1)S(1)}, f32[4,64]{1,0:T(4,128)S(1)}) custom-call(f32[4,1,2048,2048]{3,2,1,0:T(8,128)} %snap_ref.1, s32[4]{0:T(128)} %steps_hbm.1, s32[4,64]{1,0:T(4,128)} %mask_hbm.1, f32[32,128]{1,0:T(8,128)} %bitcast.1), custom_call_target="tpu_custom_call" | custom-call | flops 41943040 | bytes 75497472 | tf_op jit(solution)/shard_map/pallas_call | solution.py:309
  194.5 3.4 %shard_map.60 = (bf16[4,512,2048]{2,1,0:T(8,128)(2,1)}, f32[4,64]{1,0:T(4,128)}) custom-call(bf16[6,512,2048]{2,1,0:T(8,128)(2,1)S(1)} %get-tuple-element.4.land_ref, f32[4,64]{1,0:T(4,128)S(1)} %get-tuple-element.5.sums_ref), custom_call_target="tpu_custom_call" | custom-call | tf_op jit(solution)/shard_map/pallas_call | solution.py:355

commit v4 on v2

--- a/solution.py
+++ b/solution.py
@@ -11,9 +11,9 @@
 MESH = pl.DeviceIdType.MESH
 BLOCK = 128
 CORES = 2
-CHUNK = 32
+CHUNK = 16
 STRIP = 16
-FETCH = 3
+FETCH = 4
 decay_span = 1000.0
 
 

time: 198 us -> 201 us (1.015); the launches traced: 198 us -> 198 us
  no operation moved by 1% of the time
where the time goes in v4:
time: 201 us; the launch traced here: 198 us
  Pallas kernels  197 us (98%)
    pallas_call x1, Pallas kernels, fused(): pl.pallas_call(functools.partial(kernel, (nx, ny, nz, norm)), out_shape=(...  194 us

profile of v4, /device:TPU:12, one launch (start us, length us, event | category | flops | bytes accessed | tf_op | source)
XLA Modules:
  0.0 197.6 jit_solution(6598147176582829414)
XLA Ops:
  0.6 193.6 %shard_map.59 = (bf16[6,512,2048]{2,1,0:T(8,128)(2,1)S(1)}, f32[4,64]{1,0:T(4,128)S(1)}) custom-call(f32[4,1,2048,2048]{3,2,1,0:T(8,128)} %snap_ref.1, s32[4]{0:T(128)} %steps_hbm.1, s32[4,64]{1,0:T(4,128)} %mask_hbm.1, f32[32,128]{1,0:T(8,128)} %bitcast.1), custom_call_target="tpu_custom_call" | custom-call | flops 41943040 | bytes 75497472 | tf_op jit(solution)/shard_map/pallas_call | solution.py:295
  194.2 3.4 %shard_map.60 = (bf16[4,512,2048]{2,1,0:T(8,128)(2,1)}, f32[4,64]{1,0:T(4,128)}) custom-call(bf16[6,512,2048]{2,1,0:T(8,128)(2,1)S(1)} %get-tuple-element.4.land_ref, f32[4,64]{1,0:T(4,128)S(1)} %get-tuple-element.5.sums_ref), custom_call_target="tpu_custom_call" | custom-call | tf_op jit(solution)/shard_map/pallas_call | solution.py:341
